TPU v7x, 32 devices: a whole 2x2x4 slice. The times are simulated.
32 devices in a mesh: tm: 4 (over y, x), space: 8 (over z, core).
Axes of the slice: x: 2, y: 2, z: 4, core: 2. Of those that a mesh axis runs over, the one named last changes fastest.
Arguments:
- guess: float32 [8, 256, 4096], P('tm', 'space'), may hold values from -6 to 6
- sources: bfloat16 [32, 256, 4096], P('tm', 'space'), may hold values from -6 to 6
- velocity: bfloat16 [4, 2, 256, 4096], P(None, None, 'space'), may hold values from -1 to 1
- snapshot: int32 [32], replicated, may hold values from 0 to 3
Outputs:
- c_values: float32 [8, 256, 4096], P('tm', 'space')
- control_grad: float32 [256, 4096], P('space', 'tm')
Inputs may be any that keep to these rules, and one draw needn't show every extreme that they name: Each entry names a stored snapshot.
All inputs are finite; a program needn't handle non-finite values.
Results may differ from a plain program's by a relative error of at most 0.0003.
Values may be sent and summed in bfloat16 or wider, within the bound.
A program may use at most 128 MiB of HBM per device.

v0:
```python
import jax
import jax.numpy as jnp
import numpy as np
from jax import lax
from jax.sharding import PartitionSpec as P

FINE_DIFF = 0.2
FINE_ADV = 0.3
COARSE_DIFF = 0.24
COARSE_ADV = 0.4


def with_halo(array, sides, width):
    for axis, dim in sides:
        count, length = (lax.axis_size(axis), array.shape[dim])
        up = [(i, (i + 1) % count) for i in range(count - 1)]
        down = [(j, i) for i, j in up]
        last = lax.slice_in_dim(array, length - width, length, axis=dim)
        leading = lax.slice_in_dim(array, 0, width, axis=dim)
        before = lax.ppermute(last, axis, up)
        after = lax.ppermute(leading, axis, down)
        array = jnp.concatenate([before, array, after], axis=dim)
    return array


def passed_along(array, axis, by):
    count = lax.axis_size(axis)
    pairs = [(i, i + by) for i in range(count) if 0 <= i + by < count]
    return lax.ppermute(array, axis, pairs)


def shift_east(field):
    return jnp.concatenate([field[..., 1:], jnp.zeros_like(field[..., :1])], -1)


def shift_west(field):
    return jnp.concatenate([jnp.zeros_like(field[..., :1]), field[..., :-1]], -1)


def adjoint_step(state, speeds, diff, adv):
    speed_x = speeds[..., 0, :, :].astype(jnp.float32)
    speed_y = speeds[..., 1, :, :].astype(jnp.float32)
    centre = state[..., 1:-1, :]
    flux_x = speed_x * state
    flux_y = (speed_y * state)[..., 1:-1, :]
    laplace = (
        state[..., 2:, :]
        + state[..., :-2, :]
        + shift_east(centre)
        + shift_west(centre)
        - 4.0 * centre
    )
    advected = flux_x[..., 2:, :] - flux_x[..., :-2, :] + shift_east(flux_y) - shift_west(flux_y)
    return centre + diff * laplace + 0.5 * adv * advected


def body(guess, sources, velocity, snapshot):
    c_points, strip_rows, columns = guess.shape
    steps_dev = sources.shape[0]
    factor = steps_dev // c_points
    snap_count = velocity.shape[0]
    time_blocks = lax.axis_size("tm")
    span_no = lax.axis_index("tm")
    total_steps = steps_dev * time_blocks
    local_snap = lax.dynamic_slice_in_dim(snapshot, span_no * steps_dev, steps_dev)
    flat_speeds = velocity.reshape(snap_count * 2, strip_rows, columns)
    halo_width = 1
    speed_ext = with_halo(flat_speeds, (("space", 1),), 1)
    source_width = 0
    speed_ext = speed_ext.reshape(snap_count, 2, strip_rows + 2 * halo_width, columns)

    def rows_of(field, have, want):
        return field[..., have - want : have - want + strip_rows + 2 * want, :]

    def above(coarse_vals):
        upper = passed_along(coarse_vals[0], "tm", -1)
        return jnp.concatenate([coarse_vals[1:], upper[None]], 0)

    def relax(coarse_vals, with_residual):
        tops = above(coarse_vals)
        state = tops
        reach = 0
        time_total = jnp.zeros((strip_rows, columns), jnp.float32)
        residual = None
        last_offset = 0 if with_residual else 1
        for offset in range(factor - 1, last_offset - 1, -1):
            state = with_halo(state, (("space", 1),), 1)
            reach = 1
            positions = np.arange(c_points) * factor + offset
            picks = local_snap[positions]
            speeds = jnp.take(speed_ext, picks, axis=0)
            updated = adjoint_step(state, rows_of(speeds, halo_width, reach), FINE_DIFF, FINE_ADV)
            reach = reach - 1
            updated = updated + rows_of(sources[positions], source_width, reach).astype(jnp.float32)
            if offset == 0:
                residual = updated - coarse_vals
            else:
                time_total = time_total + jnp.sum(updated[:, reach : reach + strip_rows], 0)
            state = updated
        return (time_total, residual)

    _, residual = relax(guess, True)
    speed_one = rows_of(speed_ext, halo_width, 1)

    def coarse_step(correction, snap_pick):
        extended = with_halo(correction, (("space", 0),), 1)
        speeds = lax.dynamic_index_in_dim(speed_one, snap_pick, 0, keepdims=False)
        return adjoint_step(extended, speeds, COARSE_DIFF, COARSE_ADV)

    zero_field = jnp.zeros((strip_rows, columns), jnp.float32)
    coarse_snaps = local_snap[np.arange(c_points) * factor]

    def local_chain(correction):
        values = []
        for interval in range(c_points - 1, -1, -1):
            correction = coarse_step(correction, coarse_snaps[interval]) + residual[interval]
            values.append(correction)
        return (correction, jnp.stack(values[::-1], 0))

    def round_fn(round_no, incoming):
        lowest, _ = local_chain(incoming)
        return passed_along(lowest, "tm", -1)

    incoming = lax.fori_loop(0, time_blocks - 1, round_fn, zero_field)
    _, corr = local_chain(incoming)
    c_values = guess + corr
    f_total, _ = relax(c_values, False)
    local_total = jnp.sum(c_values, 0) + f_total
    control_grad = (
        lax.psum_scatter(local_total, "tm", scatter_dimension=1, tiled=True) / total_steps
    )
    return (c_values, control_grad)


def solution(mesh):
    in_specs = (P("tm", "space", None), P("tm", "space", None), P(None, None, "space", None), P())
    out_specs = (P("tm", "space", None), P("space", "tm"))
    return jax.shard_map(body, mesh=mesh, in_specs=in_specs, out_specs=out_specs, check_vma=False)
```

profile of v0, /device:TPU:0, one launch (start us, length us, event | category | flops | bytes accessed | tf_op | source)
XLA Modules:
  0.0 302.6 jit_solution(3594015228712616546)
XLA Ops:
  33.0 5.0 %pad_maximum_fusion.6 = bf16[4,2,34,4096]{3,1,2,0:T(2,128)(2,1)S(1)} fusion(bf16[4,2,1,4096]{3,1,2,0:T(2,128)(2,1)S(1)} %bitcast.124, bf16[4,2,32,4096]{3,1,2,0:T(2,128)(2,1)} %copy.88, bf16[4,2,1,4096]{3,1,2,0:T(2,128)(2,1)S(1)} %bitcast.123), kind=kLoop, calls=%fused_computation.46 | loop fusion | flops 2228224 | bytes 4456448 | tf_op jit(solution)/shard_map/concatenate | solution.py:22
  44.9 3.7 %gather_fusion.9 = bf16[2,2,34,4096]{3,1,2,0:T(2,128)(2,1)} fusion(bf16[4,2,34,4096]{3,1,2,0:T(2,128)(2,1)S(1)} %pad_maximum_fusion.6, s32[1024]{0:T(1024)S(1)} %pad_clamp_fusion.3), kind=kCustom, calls=%fused_computation.1.clone | custom fusion | bytes 2228232 | tf_op jit(solution)/shard_map/jit(_take)/gather | solution.py:91
  48.6 3.7 %gather_fusion.10 = bf16[2,2,34,4096]{3,1,2,0:T(2,128)(2,1)} fusion(bf16[4,2,34,4096]{3,1,2,0:T(2,128)(2,1)S(1)} %pad_maximum_fusion.6, s32[1024]{0:T(1024)S(1)} %pad_clamp_fusion.1), kind=kCustom, calls=%fused_computation.2.clone | custom fusion | bytes 2228232 | tf_op jit(solution)/shard_map/jit(_take)/gather | solution.py:91
  66.5 6.0 %collective-permute-start.9 = (f32[2,1,4096]{2,1,0:T(1,128)S(1)}, f32[2,1,4096]{2,1,0:T(1,128)S(1)}, u32[]{:S(2)}, u32[]{:S(2)}) collective-permute-start(f32[2,1,4096]{2,1,0:T(1,128)S(1)} %get-tuple-element.184), channel_id=1, source_target_pairs={{0,1},{1,2},{2,3},{3,4},{4,5},{5,6},{6,7},{8,9},{9,10},{10,11},{11... | collective-permute-start | bytes 98312 | tf_op jit(solution)/shard_map/ppermute | solution.py:20
  81.5 4.4 %collective-permute-start.11 = (f32[2,1,4096]{2,1,0:T(1,128)S(1)}, f32[2,1,4096]{2,1,0:T(1,128)S(1)}, u32[]{:S(2)}, u32[]{:S(2)}) collective-permute-start(f32[2,1,4096]{2,1,0:T(1,128)S(1)} %get-tuple-element.180), channel_id=1, source_target_pairs={{0,1},{1,2},{2,3},{3,4},{4,5},{5,6},{6,7},{8,9},{9,10},{10,11},{11... | collective-permute-start | bytes 98312 | tf_op jit(solution)/shard_map/ppermute | solution.py:20
  90.4 4.4 %collective-permute-start.13 = (f32[2,1,4096]{2,1,0:T(1,128)S(1)}, f32[2,1,4096]{2,1,0:T(1,128)S(1)}, u32[]{:S(2)}, u32[]{:S(2)}) collective-permute-start(f32[2,1,4096]{2,1,0:T(1,128)S(1)} %get-tuple-element.176), channel_id=1, source_target_pairs={{0,1},{1,2},{2,3},{3,4},{4,5},{5,6},{6,7},{8,9},{9,10},{10,11},{11... | collective-permute-start | bytes 98312 | tf_op jit(solution)/shard_map/ppermute | solution.py:20
  99.4 5.0 %collective-permute-start.15 = (f32[2,1,4096]{2,1,0:T(1,128)S(1)}, f32[2,1,4096]{2,1,0:T(1,128)S(1)}, u32[]{:S(2)}, u32[]{:S(2)}) collective-permute-start(f32[2,1,4096]{2,1,0:T(1,128)S(1)} %get-tuple-element.172), channel_id=1, source_target_pairs={{0,1},{1,2},{2,3},{3,4},{4,5},{5,6},{6,7},{8,9},{9,10},{10,11},{11... | collective-permute-start | bytes 98312 | tf_op jit(solution)/shard_map/ppermute | solution.py:20
  108.1 95.2 %while.12 = (s32[]{:T(128)}, f32[32,4096]{1,0:T(8,128)S(1)}, bf16[1,2,34,4096]{3,2,1,0:T(8,128)(2,1)S(1)}, f32[2,32,4096]{2,1,0:T(8,128)S(1)}, bf16[1,2,34,4096]{3,2,1,0:T(8,128)(2,1)S(1)}, /*index=5*/s32[]{:T(128)}) while((s32[]{:T(128)}, f32[32,4096]{1,0:T(8,128)S(1)}, bf16[1,2,34,4096]{3,2,1,0:T(8,128)(2,1)S(1)}, ...), condition=%wide.region_1.3_spmd, body=%wide.region_0.0_spmd.sunk | while | flops 5603330 | bytes 24835340 | solution.py:124
  109.4 5.0 %collective-permute-start.1 = (f32[1,4096]{1,0:T(1,128)S(1)}, f32[1,4096]{1,0:T(1,128)S(1)}, u32[]{:S(2)}, u32[]{:S(2)}) collective-permute-start(f32[1,4096]{1,0:T(1,128)S(1)} %get-tuple-element.256), channel_id=1, source_target_pairs={{0,1},{1,2},{2,3},{3,4},{4,5},{5,6},{6,7},{8,9},{9,10},{10,11},{11... | collective-permute-start | bytes 49160 | tf_op jit(solution)/shard_map/while/body/eval_jaxpr/ppermute | solution.py:20
  117.5 4.9 %collective-permute-start.3 = (f32[1,4096]{1,0:T(1,128)S(1)}, f32[1,4096]{1,0:T(1,128)S(1)}, u32[]{:S(2)}, u32[]{:S(2)}) collective-permute-start(f32[1,4096]{1,0:T(1,128)S(1)} %get-tuple-element.264), channel_id=1, source_target_pairs={{0,1},{1,2},{2,3},{3,4},{4,5},{5,6},{6,7},{8,9},{9,10},{10,11},{11... | collective-permute-start | bytes 49160 | tf_op jit(solution)/shard_map/while/body/eval_jaxpr/ppermute | solution.py:20
  125.4 14.3 %collective-permute-done.4 = f32[32,4096]{1,0:T(8,128)S(1)} collective-permute-done((f32[32,4096]{1,0:T(8,128)S(1)}, f32[32,4096]{1,0:T(8,128)S(1)}, u32[]{:S(2)}, u32[]{:S(2)}) %collective-permute-start.4) | collective-permute-done | bytes 524320 | tf_op jit(solution)/shard_map/while/body/eval_jaxpr/ppermute | solution.py:29
  141.0 4.1 %collective-permute-start.1 = (f32[1,4096]{1,0:T(1,128)S(1)}, f32[1,4096]{1,0:T(1,128)S(1)}, u32[]{:S(2)}, u32[]{:S(2)}) collective-permute-start(f32[1,4096]{1,0:T(1,128)S(1)} %get-tuple-element.256), channel_id=1, source_target_pairs={{0,1},{1,2},{2,3},{3,4},{4,5},{5,6},{6,7},{8,9},{9,10},{10,11},{11... | collective-permute-start | bytes 49160 | tf_op jit(solution)/shard_map/while/body/eval_jaxpr/ppermute | solution.py:20
  148.1 6.1 %collective-permute-start.3 = (f32[1,4096]{1,0:T(1,128)S(1)}, f32[1,4096]{1,0:T(1,128)S(1)}, u32[]{:S(2)}, u32[]{:S(2)}) collective-permute-start(f32[1,4096]{1,0:T(1,128)S(1)} %get-tuple-element.264), channel_id=1, source_target_pairs={{0,1},{1,2},{2,3},{3,4},{4,5},{5,6},{6,7},{8,9},{9,10},{10,11},{11... | collective-permute-start | bytes 49160 | tf_op jit(solution)/shard_map/while/body/eval_jaxpr/ppermute | solution.py:20
  157.2 14.3 %collective-permute-done.4 = f32[32,4096]{1,0:T(8,128)S(1)} collective-permute-done((f32[32,4096]{1,0:T(8,128)S(1)}, f32[32,4096]{1,0:T(8,128)S(1)}, u32[]{:S(2)}, u32[]{:S(2)}) %collective-permute-start.4) | collective-permute-done | bytes 524320 | tf_op jit(solution)/shard_map/while/body/eval_jaxpr/ppermute | solution.py:29
  172.8 4.1 %collective-permute-start.1 = (f32[1,4096]{1,0:T(1,128)S(1)}, f32[1,4096]{1,0:T(1,128)S(1)}, u32[]{:S(2)}, u32[]{:S(2)}) collective-permute-start(f32[1,4096]{1,0:T(1,128)S(1)} %get-tuple-element.256), channel_id=1, source_target_pairs={{0,1},{1,2},{2,3},{3,4},{4,5},{5,6},{6,7},{8,9},{9,10},{10,11},{11... | collective-permute-start | bytes 49160 | tf_op jit(solution)/shard_map/while/body/eval_jaxpr/ppermute | solution.py:20
  179.9 6.1 %collective-permute-start.3 = (f32[1,4096]{1,0:T(1,128)S(1)}, f32[1,4096]{1,0:T(1,128)S(1)}, u32[]{:S(2)}, u32[]{:S(2)}) collective-permute-start(f32[1,4096]{1,0:T(1,128)S(1)} %get-tuple-element.264), channel_id=1, source_target_pairs={{0,1},{1,2},{2,3},{3,4},{4,5},{5,6},{6,7},{8,9},{9,10},{10,11},{11... | collective-permute-start | bytes 49160 | tf_op jit(solution)/shard_map/while/body/eval_jaxpr/ppermute | solution.py:20
  189.0 14.3 %collective-permute-done.4 = f32[32,4096]{1,0:T(8,128)S(1)} collective-permute-done((f32[32,4096]{1,0:T(8,128)S(1)}, f32[32,4096]{1,0:T(8,128)S(1)}, u32[]{:S(2)}, u32[]{:S(2)}) %collective-permute-start.4) | collective-permute-done | bytes 524320 | tf_op jit(solution)/shard_map/while/body/eval_jaxpr/ppermute | solution.py:29
  204.6 4.1 %collective-permute-start.17 = (f32[1,4096]{1,0:T(1,128)S(1)}, f32[1,4096]{1,0:T(1,128)S(1)}, u32[]{:S(2)}, u32[]{:S(2)}) collective-permute-start(f32[1,4096]{1,0:T(1,128)S(1)} %get-tuple-element.200), channel_id=1, source_target_pairs={{0,1},{1,2},{2,3},{3,4},{4,5},{5,6},{6,7},{8,9},{9,10},{10,11},{11... | collective-permute-start | bytes 49160 | tf_op jit(solution)/shard_map/ppermute | solution.py:20
  211.9 5.2 %collective-permute-start.19 = (f32[1,4096]{1,0:T(1,128)S(1)}, f32[1,4096]{1,0:T(1,128)S(1)}, u32[]{:S(2)}, u32[]{:S(2)}) collective-permute-start(f32[1,4096]{1,0:T(1,128)S(1)} %get-tuple-element.196), channel_id=1, source_target_pairs={{0,1},{1,2},{2,3},{3,4},{4,5},{5,6},{6,7},{8,9},{9,10},{10,11},{11... | collective-permute-start | bytes 49160 | tf_op jit(solution)/shard_map/ppermute | solution.py:20
  221.5 14.1 %collective-permute-done.20 = f32[32,4096]{1,0:T(8,128)S(1)} collective-permute-done((f32[32,4096]{1,0:T(8,128)S(1)}, f32[32,4096]{1,0:T(8,128)S(1)}, u32[]{:S(2)}, u32[]{:S(2)}) %collective-permute-start.20) | collective-permute-done | bytes 524320 | tf_op jit(solution)/shard_map/ppermute | solution.py:29
  237.0 4.2 %collective-permute-start.22 = (f32[2,1,4096]{2,1,0:T(1,128)S(1)}, f32[2,1,4096]{2,1,0:T(1,128)S(1)}, u32[]{:S(2)}, u32[]{:S(2)}) collective-permute-start(f32[2,1,4096]{2,1,0:T(1,128)S(1)} %get-tuple-element.166), channel_id=1, source_target_pairs={{0,1},{1,2},{2,3},{3,4},{4,5},{5,6},{6,7},{8,9},{9,10},{10,11},{11... | collective-permute-start | bytes 98312 | tf_op jit(solution)/shard_map/ppermute | solution.py:20
  246.8 5.5 %collective-permute-start.24 = (f32[2,1,4096]{2,1,0:T(1,128)S(1)}, f32[2,1,4096]{2,1,0:T(1,128)S(1)}, u32[]{:S(2)}, u32[]{:S(2)}) collective-permute-start(f32[2,1,4096]{2,1,0:T(1,128)S(1)} %get-tuple-element.162), channel_id=1, source_target_pairs={{0,1},{1,2},{2,3},{3,4},{4,5},{5,6},{6,7},{8,9},{9,10},{10,11},{11... | collective-permute-start | bytes 98312 | tf_op jit(solution)/shard_map/ppermute | solution.py:20
  256.9 5.1 %collective-permute-start.26 = (f32[2,1,4096]{2,1,0:T(1,128)S(1)}, f32[2,1,4096]{2,1,0:T(1,128)S(1)}, u32[]{:S(2)}, u32[]{:S(2)}) collective-permute-start(f32[2,1,4096]{2,1,0:T(1,128)S(1)} %get-tuple-element.158), channel_id=1, source_target_pairs={{0,1},{1,2},{2,3},{3,4},{4,5},{5,6},{6,7},{8,9},{9,10},{10,11},{11... | collective-permute-start | bytes 98312 | tf_op jit(solution)/shard_map/ppermute | solution.py:20
  266.2 27.7 %reduce-scatter.2.cloned.1.call-done = f32[32,1024]{1,0:T(8,128)} async-done(((f32[32,4096]{1,0:T(8,128)}), f32[32,1024]{1,0:T(8,128)}) %reduce-scatter.2.cloned.1.call-update) | async-done | bytes 131088 | tf_op jit(solution)/shard_map/reduce_scatter | solution.py:130
  (236 shorter events, 112.1 us)
Async XLA Ops:
  7.2 286.8 %reduce-scatter.2.cloned.1.call-start = ((), (), s32[]{:S(2)}) async-start(), calls=%async_computation.1 | async-start | bytes 655360 | tf_op jit(solution)/shard_map/reduce_scatter | solution.py:130
  8.9 23.9 %collective-permute-start.5 = (bf16[8,1,4096]{2,0,1:T(8,128)(2,1)S(1)}, bf16[8,1,4096]{2,0,1:T(8,128)(2,1)S(1)}, u32[]{:S(2)}, u32[]{:S(2)}) collective-permute-start(bf16[8,1,4096]{2,0,1:T(8,128)(2,1)S(1)} %copy.102), channel_id=1, source_target_pairs={{0,1},{1,2},{2,3},{3,4},{4,5},{5,6},{6,7},{8,9},{9,10},{10,11},{11... | collective-permute-start | bytes 196616 | tf_op jit(solution)/shard_map/ppermute | solution.py:20
  11.5 21.4 %collective-permute-start.6 = (bf16[8,1,4096]{2,0,1:T(8,128)(2,1)S(1)}, bf16[8,1,4096]{2,0,1:T(8,128)(2,1)S(1)}, u32[]{:S(2)}, u32[]{:S(2)}) collective-permute-start(bf16[8,1,4096]{2,0,1:T(8,128)(2,1)S(1)} %copy.103), channel_id=1, source_target_pairs={{1,0},{2,1},{3,2},{4,3},{5,4},{6,5},{7,6},{9,8},{10,9},{11,10},{12... | collective-permute-start | bytes 196616 | tf_op jit(solution)/shard_map/ppermute | solution.py:21
  15.2 49.0 %collective-permute-start.7 = (f32[32,4096]{1,0:T(8,128)}, f32[32,4096]{1,0:T(8,128)}, u32[]{:S(2)}, u32[]{:S(2)}) collective-permute-start(f32[32,4096]{1,0:T(8,128)} %get-tuple-element.186), channel_id=1, source_target_pairs={{8,0},{16,8},{24,16},{9,1},{17,9},{25,17},{10,2},{18,10},{26,18},{... | collective-permute-start | bytes 1572872 | tf_op jit(solution)/shard_map/ppermute | solution.py:29
  65.2 8.9 %collective-permute-start.8 = (f32[2,1,4096]{2,1,0:T(1,128)S(1)}, f32[2,1,4096]{2,1,0:T(1,128)S(1)}, u32[]{:S(2)}, u32[]{:S(2)}) collective-permute-start(f32[2,1,4096]{2,1,0:T(1,128)S(1)} %get-tuple-element.185), channel_id=1, source_target_pairs={{1,0},{2,1},{3,2},{4,3},{5,4},{6,5},{7,6},{9,8},{10,9},{11,10},{12... | collective-permute-start | bytes 98312 | tf_op jit(solution)/shard_map/ppermute | solution.py:21
  66.5 7.6 %collective-permute-start.9 = (f32[2,1,4096]{2,1,0:T(1,128)S(1)}, f32[2,1,4096]{2,1,0:T(1,128)S(1)}, u32[]{:S(2)}, u32[]{:S(2)}) collective-permute-start(f32[2,1,4096]{2,1,0:T(1,128)S(1)} %get-tuple-element.184), channel_id=1, source_target_pairs={{0,1},{1,2},{2,3},{3,4},{4,5},{5,6},{6,7},{8,9},{9,10},{10,11},{11... | collective-permute-start | bytes 98312 | tf_op jit(solution)/shard_map/ppermute | solution.py:20
  80.2 6.1 %collective-permute-start.10 = (f32[2,1,4096]{2,1,0:T(1,128)S(1)}, f32[2,1,4096]{2,1,0:T(1,128)S(1)}, u32[]{:S(2)}, u32[]{:S(2)}) collective-permute-start(f32[2,1,4096]{2,1,0:T(1,128)S(1)} %get-tuple-element.181), channel_id=1, source_target_pairs={{1,0},{2,1},{3,2},{4,3},{5,4},{6,5},{7,6},{9,8},{10,9},{11,10},{12... | collective-permute-start | bytes 98312 | tf_op jit(solution)/shard_map/ppermute | solution.py:21
  89.1 6.1 %collective-permute-start.12 = (f32[2,1,4096]{2,1,0:T(1,128)S(1)}, f32[2,1,4096]{2,1,0:T(1,128)S(1)}, u32[]{:S(2)}, u32[]{:S(2)}) collective-permute-start(f32[2,1,4096]{2,1,0:T(1,128)S(1)} %get-tuple-element.177), channel_id=1, source_target_pairs={{1,0},{2,1},{3,2},{4,3},{5,4},{6,5},{7,6},{9,8},{10,9},{11,10},{12... | collective-permute-start | bytes 98312 | tf_op jit(solution)/shard_map/ppermute | solution.py:21
  98.1 6.7 %collective-permute-start.14 = (f32[2,1,4096]{2,1,0:T(1,128)S(1)}, f32[2,1,4096]{2,1,0:T(1,128)S(1)}, u32[]{:S(2)}, u32[]{:S(2)}) collective-permute-start(f32[2,1,4096]{2,1,0:T(1,128)S(1)} %get-tuple-element.173), channel_id=1, source_target_pairs={{1,0},{2,1},{3,2},{4,3},{5,4},{6,5},{7,6},{9,8},{10,9},{11,10},{12... | collective-permute-start | bytes 98312 | tf_op jit(solution)/shard_map/ppermute | solution.py:21
  108.1 6.5 %collective-permute-start = (f32[1,4096]{1,0:T(1,128)S(1)}, f32[1,4096]{1,0:T(1,128)S(1)}, u32[]{:S(2)}, u32[]{:S(2)}) collective-permute-start(f32[1,4096]{1,0:T(1,128)S(1)} %get-tuple-element.255), channel_id=1, source_target_pairs={{1,0},{2,1},{3,2},{4,3},{5,4},{6,5},{7,6},{9,8},{10,9},{11,10},{12... | collective-permute-start | bytes 49160 | tf_op jit(solution)/shard_map/while/body/eval_jaxpr/ppermute | solution.py:21
  116.2 6.4 %collective-permute-start.2 = (f32[1,4096]{1,0:T(1,128)S(1)}, f32[1,4096]{1,0:T(1,128)S(1)}, u32[]{:S(2)}, u32[]{:S(2)}) collective-permute-start(f32[1,4096]{1,0:T(1,128)S(1)} %get-tuple-element.263), channel_id=1, source_target_pairs={{1,0},{2,1},{3,2},{4,3},{5,4},{6,5},{7,6},{9,8},{10,9},{11,10},{12... | collective-permute-start | bytes 49160 | tf_op jit(solution)/shard_map/while/body/eval_jaxpr/ppermute | solution.py:21
  124.1 15.6 %collective-permute-start.4 = (f32[32,4096]{1,0:T(8,128)S(1)}, f32[32,4096]{1,0:T(8,128)S(1)}, u32[]{:S(2)}, u32[]{:S(2)}) collective-permute-start(f32[32,4096]{1,0:T(8,128)S(1)} %fusion.177), channel_id=1, source_target_pairs={{8,0},{16,8},{24,16},{9,1},{17,9},{25,17},{10,2},{18,10},{26,18},{... | collective-permute-start | bytes 1572872 | tf_op jit(solution)/shard_map/while/body/eval_jaxpr/ppermute | solution.py:29
  146.8 7.6 %collective-permute-start.2 = (f32[1,4096]{1,0:T(1,128)S(1)}, f32[1,4096]{1,0:T(1,128)S(1)}, u32[]{:S(2)}, u32[]{:S(2)}) collective-permute-start(f32[1,4096]{1,0:T(1,128)S(1)} %get-tuple-element.263), channel_id=1, source_target_pairs={{1,0},{2,1},{3,2},{4,3},{5,4},{6,5},{7,6},{9,8},{10,9},{11,10},{12... | collective-permute-start | bytes 49160 | tf_op jit(solution)/shard_map/while/body/eval_jaxpr/ppermute | solution.py:21
  148.1 6.9 %collective-permute-start.3 = (f32[1,4096]{1,0:T(1,128)S(1)}, f32[1,4096]{1,0:T(1,128)S(1)}, u32[]{:S(2)}, u32[]{:S(2)}) collective-permute-start(f32[1,4096]{1,0:T(1,128)S(1)} %get-tuple-element.264), channel_id=1, source_target_pairs={{0,1},{1,2},{2,3},{3,4},{4,5},{5,6},{6,7},{8,9},{9,10},{10,11},{11... | collective-permute-start | bytes 49160 | tf_op jit(solution)/shard_map/while/body/eval_jaxpr/ppermute | solution.py:20
  155.9 15.6 %collective-permute-start.4 = (f32[32,4096]{1,0:T(8,128)S(1)}, f32[32,4096]{1,0:T(8,128)S(1)}, u32[]{:S(2)}, u32[]{:S(2)}) collective-permute-start(f32[32,4096]{1,0:T(8,128)S(1)} %fusion.177), channel_id=1, source_target_pairs={{8,0},{16,8},{24,16},{9,1},{17,9},{25,17},{10,2},{18,10},{26,18},{... | collective-permute-start | bytes 1572872 | tf_op jit(solution)/shard_map/while/body/eval_jaxpr/ppermute | solution.py:29
  178.6 7.6 %collective-permute-start.2 = (f32[1,4096]{1,0:T(1,128)S(1)}, f32[1,4096]{1,0:T(1,128)S(1)}, u32[]{:S(2)}, u32[]{:S(2)}) collective-permute-start(f32[1,4096]{1,0:T(1,128)S(1)} %get-tuple-element.263), channel_id=1, source_target_pairs={{1,0},{2,1},{3,2},{4,3},{5,4},{6,5},{7,6},{9,8},{10,9},{11,10},{12... | collective-permute-start | bytes 49160 | tf_op jit(solution)/shard_map/while/body/eval_jaxpr/ppermute | solution.py:21
  179.9 6.9 %collective-permute-start.3 = (f32[1,4096]{1,0:T(1,128)S(1)}, f32[1,4096]{1,0:T(1,128)S(1)}, u32[]{:S(2)}, u32[]{:S(2)}) collective-permute-start(f32[1,4096]{1,0:T(1,128)S(1)} %get-tuple-element.264), channel_id=1, source_target_pairs={{0,1},{1,2},{2,3},{3,4},{4,5},{5,6},{6,7},{8,9},{9,10},{10,11},{11... | collective-permute-start | bytes 49160 | tf_op jit(solution)/shard_map/while/body/eval_jaxpr/ppermute | solution.py:20
  187.7 15.6 %collective-permute-start.4 = (f32[32,4096]{1,0:T(8,128)S(1)}, f32[32,4096]{1,0:T(8,128)S(1)}, u32[]{:S(2)}, u32[]{:S(2)}) collective-permute-start(f32[32,4096]{1,0:T(8,128)S(1)} %fusion.177), channel_id=1, source_target_pairs={{8,0},{16,8},{24,16},{9,1},{17,9},{25,17},{10,2},{18,10},{26,18},{... | collective-permute-start | bytes 1572872 | tf_op jit(solution)/shard_map/while/body/eval_jaxpr/ppermute | solution.py:29
  210.4 6.8 %collective-permute-start.18 = (f32[1,4096]{1,0:T(1,128)S(1)}, f32[1,4096]{1,0:T(1,128)S(1)}, u32[]{:S(2)}, u32[]{:S(2)}) collective-permute-start(f32[1,4096]{1,0:T(1,128)S(1)} %get-tuple-element.197), channel_id=1, source_target_pairs={{1,0},{2,1},{3,2},{4,3},{5,4},{6,5},{7,6},{9,8},{10,9},{11,10},{12... | collective-permute-start | bytes 49160 | tf_op jit(solution)/shard_map/ppermute | solution.py:21
  211.9 6.0 %collective-permute-start.19 = (f32[1,4096]{1,0:T(1,128)S(1)}, f32[1,4096]{1,0:T(1,128)S(1)}, u32[]{:S(2)}, u32[]{:S(2)}) collective-permute-start(f32[1,4096]{1,0:T(1,128)S(1)} %get-tuple-element.196), channel_id=1, source_target_pairs={{0,1},{1,2},{2,3},{3,4},{4,5},{5,6},{6,7},{8,9},{9,10},{10,11},{11... | collective-permute-start | bytes 49160 | tf_op jit(solution)/shard_map/ppermute | solution.py:20
  220.0 15.6 %collective-permute-start.20 = (f32[32,4096]{1,0:T(8,128)S(1)}, f32[32,4096]{1,0:T(8,128)S(1)}, u32[]{:S(2)}, u32[]{:S(2)}) collective-permute-start(f32[32,4096]{1,0:T(8,128)S(1)} %get-tuple-element.168), channel_id=1, source_target_pairs={{8,0},{16,8},{24,16},{9,1},{17,9},{25,17},{10,2},{18,10},{26,18},{... | collective-permute-start | bytes 1572872 | tf_op jit(solution)/shard_map/ppermute | solution.py:29
  245.5 7.1 %collective-permute-start.23 = (f32[2,1,4096]{2,1,0:T(1,128)S(1)}, f32[2,1,4096]{2,1,0:T(1,128)S(1)}, u32[]{:S(2)}, u32[]{:S(2)}) collective-permute-start(f32[2,1,4096]{2,1,0:T(1,128)S(1)} %get-tuple-element.163), channel_id=1, source_target_pairs={{1,0},{2,1},{3,2},{4,3},{5,4},{6,5},{7,6},{9,8},{10,9},{11,10},{12... | collective-permute-start | bytes 98312 | tf_op jit(solution)/shard_map/ppermute | solution.py:21
  246.8 6.3 %collective-permute-start.24 = (f32[2,1,4096]{2,1,0:T(1,128)S(1)}, f32[2,1,4096]{2,1,0:T(1,128)S(1)}, u32[]{:S(2)}, u32[]{:S(2)}) collective-permute-start(f32[2,1,4096]{2,1,0:T(1,128)S(1)} %get-tuple-element.162), channel_id=1, source_target_pairs={{0,1},{1,2},{2,3},{3,4},{4,5},{5,6},{6,7},{8,9},{9,10},{10,11},{11... | collective-permute-start | bytes 98312 | tf_op jit(solution)/shard_map/ppermute | solution.py:20
  255.6 6.8 %collective-permute-start.25 = (f32[2,1,4096]{2,1,0:T(1,128)S(1)}, f32[2,1,4096]{2,1,0:T(1,128)S(1)}, u32[]{:S(2)}, u32[]{:S(2)}) collective-permute-start(f32[2,1,4096]{2,1,0:T(1,128)S(1)} %get-tuple-element.159), channel_id=1, source_target_pairs={{1,0},{2,1},{3,2},{4,3},{5,4},{6,5},{7,6},{9,8},{10,9},{11,10},{12... | collective-permute-start | bytes 98312 | tf_op jit(solution)/shard_map/ppermute | solution.py:21
  (42 other events, 282.0 us)
Sparse Core Ops, SparseCore 0:
  266.3 27.5 reduce-scatter.1
where the time goes:
time: 308 us; the launch traced here: 303 us
  starting transfers between devices  104 us (34%)
  waiting for transfers between devices  92.4 us (30%)
  local copies, waits for them, and re-layouts  45.6 us (15%)
  other arithmetic  41.3 us (13%)
  between operations  19 us (6%)
    ppermute x16, starting transfers between devices, with_halo(): before = lax.ppermute(last, axis, up)  76.6 us
    ppermute x5, waiting for transfers between devices, passed_along(): return lax.ppermute(array, axis, pairs)  57 us
    reduce_scatter x1, waiting for transfers between devices, body(): lax.psum_scatter(local_total, 'tm', scatter_dimension=1, tiled=True)  27.7 us
    ppermute x16, starting transfers between devices, with_halo(): after = lax.ppermute(leading, axis, down)  20.8 us
    gather x4, local copies, waits for them, and re-layouts, relax(): speeds = jnp.take(speed_ext, picks, axis=0)  13.6 us
    unnamed x60, local copies, waits for them, and re-layouts  9.75 us
    ppermute x16, waiting for transfers between devices, with_halo(): before = lax.ppermute(last, axis, up)  7.58 us
    slice x28, local copies, waits for them, and re-layouts, shift_east(): return jnp.concatenate([field[..., 1:], jnp.zeros_like(field[..., :1])], -1)  7.56 us
  transfers between devices with their start and end apart: 38, of which 19 were waited for; matrix products, arithmetic and copies ran while one was open for 17% of the time, Pallas kernels for 0%

commit v1 on v0

v1 whole, which is shorter than its diff:
```python
import functools

import jax
import jax.numpy as jnp
from jax import lax
from jax.experimental import pallas as pl
from jax.experimental.pallas import tpu as pltpu
from jax.sharding import PartitionSpec as P

FINE = (0.2, 0.15)
COARSE = (0.24, 0.2)
LANE = 128


def kernel(
    blocks,
    strips,
    snap_ref,
    guess_ref,
    src_ref,
    vel_ref,
    cval_ref,
    grad_ref,
    x_buf,
    next_guess,
    res_buf,
    b_buf,
    gathered,
    solved,
    incoming,
    corr_buf,
    total,
    totals_in,
    edge_out,
    edge_in,
    edge_send,
    edge_recv,
    big_send,
    big_recv,
):
    points, rows, cols = guess_ref.shape
    steps = src_ref.shape[0]
    factor = steps // points
    part = cols // blocks
    width = min(512, part)
    t = lax.axis_index("tm")
    s = lax.axis_index("space")
    has_up = s > 0
    has_down = s < strips - 1
    f32 = jnp.float32

    barrier = pltpu.get_barrier_semaphore()
    for d in range(1, blocks):
        pl.semaphore_signal(barrier, 1, device_id={"tm": lax.rem(t + d, blocks)})

    @pl.when(has_up)
    def _():
        pl.semaphore_signal(barrier, 1, device_id={"space": s - 1})

    @pl.when(has_down)
    def _():
        pl.semaphore_signal(barrier, 1, device_id={"space": s + 1})

    def clear_margin(ref, size):
        zero = jnp.zeros((rows, LANE), f32)
        ref[:, 0:LANE] = zero
        ref[:, size - LANE : size] = zero

    for c in range(points):
        for slot in range(2):
            clear_margin(x_buf.at[c, slot], cols + 2 * LANE)
        clear_margin(res_buf.at[c], cols + 2 * LANE)
        clear_margin(corr_buf.at[c], cols + 2 * LANE)
    clear_margin(next_guess, cols + 2 * LANE)
    clear_margin(b_buf, cols + 2 * LANE)
    clear_margin(incoming, cols + 2 * LANE)
    for i in range(blocks):
        clear_margin(gathered.at[i], part + 4 * LANE)
        for slot in range(2):
            clear_margin(solved.at[i, slot], part + 4 * LANE)
    rounds = edge_in.shape[0]

    @pl.when(jnp.logical_not(has_up))
    def _():
        def zero_top(i, carry):
            edge_in[i, 0] = jnp.zeros((1, cols), f32)
            return carry

        lax.fori_loop(0, rounds, zero_top, 0)

    @pl.when(jnp.logical_not(has_down))
    def _():
        def zero_bottom(i, carry):
            edge_in[i, 1] = jnp.zeros((1, cols), f32)
            return carry

        lax.fori_loop(0, rounds, zero_bottom, 0)

    def over_columns(fn):
        def step(k, carry):
            fn(pl.multiple_of(k * width, width))
            return carry

        lax.fori_loop(0, cols // width, step, 0)

    @pl.when(t == blocks - 1)
    def _():
        def clear(at):
            next_guess[:, pl.ds(at + LANE, width)] = jnp.zeros((rows, width), f32)
            incoming[:, pl.ds(at + LANE, width)] = jnp.zeros((rows, width), f32)

        over_columns(clear)

    peers = blocks - 1 + jnp.minimum(s, 1) + jnp.minimum(strips - 1 - s, 1)
    pl.semaphore_wait(barrier, peers)

    def edge_copies(idx, span):
        window = pl.ds(0, span)
        return (
            pltpu.make_async_remote_copy(
                edge_out.at[idx, 0, :, window],
                edge_in.at[idx, 1, :, window],
                edge_send.at[idx, 0],
                edge_recv.at[idx, 1],
                device_id={"space": s - 1},
            ),
            pltpu.make_async_remote_copy(
                edge_out.at[idx, 1, :, window],
                edge_in.at[idx, 0, :, window],
                edge_send.at[idx, 1],
                edge_recv.at[idx, 0],
                device_id={"space": s + 1},
            ),
        )

    used = []

    def send_edges(idx, span):
        used.append((idx, span))
        up, down = edge_copies(idx, span)

        @pl.when(has_up)
        def _():
            up.start()

        @pl.when(has_down)
        def _():
            down.start()

    def wait_edges(idx, span):
        up, down = edge_copies(idx, span)

        @pl.when(has_up)
        def _():
            down.wait_recv()

        @pl.when(has_down)
        def _():
            up.wait_recv()

    counter = [0]

    def new_edge():
        counter[0] += 1
        return counter[0] - 1

    def speed(snap, comp, at, size):
        return vel_ref[snap, comp, :, pl.ds(at, size)].astype(f32)

    row_no = lax.broadcasted_iota(jnp.int32, (rows, 1), 0)

    def stencil(src, at, vel_at, left_at, right_at, size, snap, kind, idx, edge_at):
        nu, h = kind
        p = src[:, pl.ds(at, size)]
        p_left = src[:, pl.ds(at - LANE, LANE)]
        p_right = src[:, pl.ds(at + size, LANE)]
        hay = h * speed(snap, 1, vel_at, size)
        hay_left = h * speed(snap, 1, left_at, LANE)
        hay_right = h * speed(snap, 1, right_at, LANE)
        hax = h * speed(snap, 0, vel_at, size)
        east = jnp.concatenate([(nu + hay) * p, (nu + hay_right) * p_right], 1)
        east = pltpu.roll(east, size + LANE - 1, 1)[:, :size]
        west = jnp.concatenate([(nu - hay_left) * p_left, (nu - hay) * p], 1)
        west = pltpu.roll(west, 1, 1)[:, LANE:]
        below = pltpu.roll((nu + hax) * p, rows - 1, 0)
        below = jnp.where(row_no == rows - 1, edge_in[idx, 1, :, pl.ds(edge_at, size)], below)
        above = pltpu.roll((nu - hax) * p, 1, 0)
        above = jnp.where(row_no == 0, edge_in[idx, 0, :, pl.ds(edge_at, size)], above)
        return (1.0 - 4.0 * nu) * p + (east + west) + (below + above)

    def put_edges(value, vel_at, size, snap, kind, idx, edge_at):
        nu, h = kind
        first = vel_ref[snap, 0, 0:16, pl.ds(vel_at, size)].astype(f32)[0:1]
        last = vel_ref[snap, 0, rows - 16 : rows, pl.ds(vel_at, size)].astype(f32)[15:16]
        edge_out[idx, 0, :, pl.ds(edge_at, size)] = (nu + h * first) * value[0:1]
        edge_out[idx, 1, :, pl.ds(edge_at, size)] = (nu - h * last) * value[rows - 1 : rows]

    def snap_at(local):
        return snap_ref[t * steps + local]

    def full_stencil(src, at, snap, kind, idx):
        left = pl.multiple_of(jnp.maximum(at - LANE, 0), LANE)
        right = pl.multiple_of(jnp.minimum(at + width, cols - LANE), LANE)
        return stencil(src, at + LANE, at, left, right, width, snap, kind, idx, at)

    def guess_copy():
        return pltpu.make_async_remote_copy(
            guess_ref.at[0],
            next_guess.at[:, pl.ds(LANE, cols)],
            big_send.at[0, 0],
            big_recv.at[0, 0],
            device_id={"tm": t - 1},
        )

    @pl.when(t > 0)
    def _():
        guess_copy().start()

    def relax_chain(c, make_src, finish_last, with_residual, accumulate):
        src = make_src()
        idx = new_edge()
        snap = snap_at(c * factor + factor - 1)

        def first(at):
            put_edges(src[:, pl.ds(at + LANE, width)], at, width, snap, FINE, idx, at)

        over_columns(first)
        send_edges(idx, cols)
        yield
        slot = 1
        last = 0 if with_residual else 1
        for offset in range(factor - 1, last - 1, -1):
            n = c * factor + offset
            snap = snap_at(n)
            dst = x_buf.at[c, slot]
            more = offset > last
            nxt = new_edge() if more else None
            snap_next = snap_at(n - 1) if more else None
            wait_edges(idx, cols)

            def work(at, src=src, dst=dst, idx=idx, nxt=nxt, snap=snap, snap_next=snap_next, n=n, offset=offset, more=more):
                new = full_stencil(src, at, snap, FINE, idx)
                new = new + src_ref[n, :, pl.ds(at, width)].astype(f32)
                if more:
                    put_edges(new, at, width, snap_next, FINE, nxt, at)
                    dst[:, pl.ds(at + LANE, width)] = new
                if accumulate:
                    total[:, pl.ds(at, width)] += new
                if offset == 0:
                    finish_last(at, new)

            over_columns(work)
            if more:
                send_edges(nxt, cols)
            src, idx, slot = dst, nxt, 1 - slot
            yield

    def run(chains):
        chains = list(chains)
        while chains:
            alive = []
            for chain in chains:
                try:
                    next(chain)
                    alive.append(chain)
                except StopIteration:
                    pass
            chains = alive

    first_coarse = new_edge()
    snap_coarse = [snap_at(c * factor) for c in range(points)]

    def first_src(c):
        def make():
            if c < points - 1:

                def fill(at):
                    x_buf[c, 0, :, pl.ds(at + LANE, width)] = guess_ref[c + 1, :, pl.ds(at, width)]

                over_columns(fill)
                return x_buf.at[c, 0]

            @pl.when(t < blocks - 1)
            def _():
                guess_copy().wait_recv()

            return next_guess

        return make

    def first_last(c):
        def finish(at, new):
            value = new - guess_ref[c, :, pl.ds(at, width)]
            res_buf[c, :, pl.ds(at + LANE, width)] = value
            if c == points - 1 and points > 1:
                put_edges(value, at, width, snap_coarse[points - 2], COARSE, first_coarse, at)
            if points == 1:
                b_buf[:, pl.ds(at + LANE, width)] = value

        return finish

    for c in range(points - 1):
        run([relax_chain(c, first_src(c), first_last(c), True, False)])
    run([relax_chain(points - 1, first_src(points - 1), first_last(points - 1), True, False)])

    src, idx = res_buf.at[points - 1], first_coarse
    if points > 1:
        send_edges(idx, cols)
    for i in range(points - 2, -1, -1):
        nxt = new_edge() if i > 0 else None
        dst = b_buf if i == 0 else x_buf.at[0, i % 2]
        wait_edges(idx, cols)

        def condense(at, src=src, dst=dst, idx=idx, nxt=nxt, i=i):
            new = full_stencil(src, at, snap_coarse[i], COARSE, idx)
            new = new + res_buf[i, :, pl.ds(at + LANE, width)]
            dst[:, pl.ds(at + LANE, width)] = new
            if i > 0:
                put_edges(new, at, width, snap_coarse[i - 1], COARSE, nxt, at)

        over_columns(condense)
        if i > 0:
            send_edges(nxt, cols)
        src, idx = dst, nxt

    wide = part + 2 * LANE

    def slab_copy(to, sender):
        return pltpu.make_async_remote_copy(
            b_buf.at[:, pl.ds(pl.multiple_of(to * part, LANE), wide)],
            gathered.at[sender, :, pl.ds(LANE, wide)],
            big_send.at[1, to],
            big_recv.at[1, sender],
            device_id={"tm": to},
        )

    @pl.when(t > 0)
    def _():
        for to in range(blocks):

            @pl.when(t != to)
            def _():
                slab_copy(to, t).start()

        for at in range(0, wide, LANE):
            gathered[t, :, at + LANE : at + 2 * LANE] = b_buf[
                :, pl.ds(pl.multiple_of(t * part + at, LANE), LANE)
            ]

    def incoming_copy(block, ref, sender):
        return pltpu.make_async_remote_copy(
            ref.at[:, pl.ds(2 * LANE, part)],
            incoming.at[:, pl.ds(pl.multiple_of(LANE + sender * part, LANE), part)],
            big_send.at[2, block],
            big_recv.at[2, sender],
            device_id={"tm": block},
        )

    pieces = [(0, LANE)]
    pieces += [(LANE + k * width, width) for k in range(part // width)]
    pieces += [(LANE + part, LANE)]
    base = t * part - LANE

    def clip(at):
        return pl.multiple_of(jnp.clip(base + at, 0, cols - LANE), LANE)

    def piece_vel(at, size):
        if size == LANE:
            return clip(at)
        return pl.multiple_of(base + at, LANE)

    def need(block):
        @pl.when(t != block)
        def _():
            slab_copy(t, block).wait_recv()

    def deliver(block, ref):
        @pl.when(t != block)
        def _():
            incoming_copy(block, ref, t).start()

        @pl.when(t == block)
        def _():
            for at in range(0, part, LANE):
                incoming[:, pl.ds(pl.multiple_of(LANE + t * part + at, LANE), LANE)] = ref[
                    :, 2 * LANE + at : 3 * LANE + at
                ]

    need(blocks - 1)
    src = gathered.at[blocks - 1]
    delivered = []
    if blocks > 1:
        deliver(blocks - 2, src)
        delivered.append((blocks - 2, src))
    chain = [(block, i) for block in range(blocks - 2, 0, -1) for i in range(points - 1, -1, -1)]

    def part_snap(block, i):
        return snap_ref[(block * points + i) * factor]

    if chain:
        idx = new_edge()
        for at, size in pieces:
            put_edges(src[:, at + LANE : at + LANE + size], piece_vel(at, size), size, part_snap(*chain[0]), COARSE, idx, at)
        send_edges(idx, wide)
    for number, (block, i) in enumerate(chain):
        more = number + 1 < len(chain)
        nxt = new_edge() if more else None
        dst = solved.at[block, i % 2]
        if i == 0:
            need(block)
        wait_edges(idx, wide)
        for at, size in pieces:
            new = stencil(
                src, at + LANE, piece_vel(at, size), clip(at - LANE), clip(at + size), size,
                part_snap(block, i), COARSE, idx, at,
            )
            if i == 0:
                new = new + gathered[block, :, at + LANE : at + LANE + size]
            if at == 0:
                new = jnp.where(t > 0, new, 0.0)
            if at == LANE + part:
                new = jnp.where(t < blocks - 1, new, 0.0)
            dst[:, at + LANE : at + LANE + size] = new
            if more:
                put_edges(new, piece_vel(at, size), size, part_snap(*chain[number + 1]), COARSE, nxt, at)
        if more:
            send_edges(nxt, wide)
        if i == 0:
            deliver(block - 1, dst)
            delivered.append((block - 1, dst))
        src, idx = dst, nxt

    for sender in range(blocks):

        @pl.when(jnp.logical_and(t < blocks - 1, t != sender))
        def _():
            incoming_copy(t, gathered.at[0], sender).wait_recv()

    ready = set()
    idx_corr = new_edge()

    def start_all(at):
        value = incoming[:, pl.ds(at + LANE, width)]
        put_edges(value, at, width, snap_coarse[points - 1], COARSE, idx_corr, at)
        x_buf[points - 1, 0, :, pl.ds(at + LANE, width)] = value + next_guess[:, pl.ds(at + LANE, width)]
        total[:, pl.ds(at, width)] = jnp.zeros((rows, width), f32)

    over_columns(start_all)
    send_edges(idx_corr, cols)

    def correction_chain():
        src, idx = incoming, idx_corr
        for i in range(points - 1, -1, -1):
            nxt = new_edge() if i > 0 else None
            dst = corr_buf.at[i]
            wait_edges(idx, cols)

            def work(at, src=src, dst=dst, idx=idx, nxt=nxt, i=i):
                new = full_stencil(src, at, snap_coarse[i], COARSE, idx)
                new = new + res_buf[i, :, pl.ds(at + LANE, width)]
                value = guess_ref[i, :, pl.ds(at, width)] + new
                cval_ref[i, :, pl.ds(at, width)] = value
                total[:, pl.ds(at, width)] += value
                if i > 0:
                    dst[:, pl.ds(at + LANE, width)] = new
                    put_edges(new, at, width, snap_coarse[i - 1], COARSE, nxt, at)
                    x_buf[i - 1, 0, :, pl.ds(at + LANE, width)] = value

            over_columns(work)
            if i > 0:
                send_edges(nxt, cols)
                ready.add(i - 1)
            src, idx = dst, nxt
            yield

    def second_chain(c):
        while c < points - 1 and c not in ready:
            yield
        yield from relax_chain(c, lambda: x_buf.at[c, 0], None, False, True)

    run([second_chain(points - 1), correction_chain()] + [second_chain(c) for c in range(points - 2, -1, -1)])

    def total_copy(to, sender):
        return pltpu.make_async_remote_copy(
            total.at[:, pl.ds(pl.multiple_of(to * part, LANE), part)],
            totals_in.at[sender],
            big_send.at[3, to],
            big_recv.at[3, sender],
            device_id={"tm": to},
        )

    for to in range(blocks):

        @pl.when(t != to)
        def _():
            total_copy(to, t).start()

    for idx, span in used:
        up, down = edge_copies(idx, span)

        @pl.when(has_up)
        def _():
            up.wait_send()

        @pl.when(has_down)
        def _():
            down.wait_send()

    @pl.when(t > 0)
    def _():
        guess_copy().wait_send()
        for to in range(blocks):

            @pl.when(t != to)
            def _():
                slab_copy(to, t).wait_send()

    for block, ref in delivered:

        @pl.when(t != block)
        def _():
            incoming_copy(block, ref, t).wait_send()

    for other in range(blocks):

        @pl.when(t != other)
        def _():
            total_copy(t, other).wait_recv()

    scale = 1.0 / (steps * blocks)
    for at in range(0, part, width):
        own = total[:, pl.ds(pl.multiple_of(t * part + at, LANE), width)]
        for other in range(blocks):
            got = totals_in[other, :, at : at + width]
            own = own + jnp.where(t == other, 0.0, got)
        grad_ref[:, at : at + width] = own * scale
    for to in range(blocks):

        @pl.when(t != to)
        def _():
            total_copy(to, t).wait_send()


def body(blocks, strips, guess, sources, velocity, snapshot):
    points, rows, cols = guess.shape
    steps = sources.shape[0]
    factor = steps // points
    part = cols // blocks
    padded = cols + 2 * LANE
    edges = points * (2 * factor + 1) + 2 * points + points * blocks
    f32 = jnp.float32
    vmem = pl.BlockSpec(memory_space=pltpu.VMEM)
    return pl.pallas_call(
        functools.partial(kernel, blocks, strips),
        out_shape=(
            jax.ShapeDtypeStruct((points, rows, cols), f32),
            jax.ShapeDtypeStruct((rows, part), f32),
        ),
        in_specs=[pl.BlockSpec(memory_space=pltpu.SMEM), vmem, vmem, vmem],
        out_specs=(vmem, vmem),
        scratch_shapes=[
            pltpu.VMEM((points, 2, rows, padded), f32),
            pltpu.VMEM((rows, padded), f32),
            pltpu.VMEM((points, rows, padded), f32),
            pltpu.VMEM((rows, padded), f32),
            pltpu.VMEM((blocks, rows, part + 4 * LANE), f32),
            pltpu.VMEM((blocks, 2, rows, part + 4 * LANE), f32),
            pltpu.VMEM((rows, padded), f32),
            pltpu.VMEM((points, rows, padded), f32),
            pltpu.VMEM((rows, cols), f32),
            pltpu.VMEM((blocks, rows, part), f32),
            pltpu.VMEM((edges, 2, 1, cols), f32),
            pltpu.VMEM((edges, 2, 1, cols), f32),
            pltpu.SemaphoreType.DMA((edges, 2)),
            pltpu.SemaphoreType.DMA((edges, 2)),
            pltpu.SemaphoreType.DMA((4, blocks)),
            pltpu.SemaphoreType.DMA((4, blocks)),
        ],
        compiler_params=pltpu.CompilerParams(
            collective_id=0, has_side_effects=True, vmem_limit_bytes=56 * 1024 * 1024
        ),
    )(snapshot, guess, sources, velocity)


def solution(mesh):
    in_specs = (P("tm", "space", None), P("tm", "space", None), P(None, None, "space", None), P())
    out_specs = (P("tm", "space", None), P("space", "tm"))
    fn = functools.partial(body, mesh.shape["tm"], mesh.shape["space"])
    return jax.shard_map(fn, mesh=mesh, in_specs=in_specs, out_specs=out_specs, check_vma=False)
```

time: 308 us -> 85.8 us (0.28); the launches traced: 303 us -> 85.5 us
  starting transfers between devices: 104 us -> 0 us
  waiting for transfers between devices: 92.4 us -> 0 us
  Pallas kernels: 0 us -> 81.8 us
  local copies, waits for them, and re-layouts: 45.6 us -> 2.96 us
  other arithmetic: 41.3 us -> 0 us
  between operations: 19 us -> 0.65 us
    ppermute x37 -> x0, starting transfers between devices: 104 us -> none  [the longest x16 76.6 us: with_halo(): before = lax.ppermute(last, axis, up)]
    pallas_call x0 -> x1, Pallas kernels: none -> 81.8 us  [body(): pl.pallas_call(functools.partial(kernel, blocks, strips), out_shape=(jax....]
    ppermute x37 -> x0, waiting for transfers between devices: 64.6 us -> none  [the longest x5 57 us: passed_along(): return lax.ppermute(array, axis, pairs)]
    reduce_scatter x1 -> x0, waiting for transfers between devices: 27.7 us -> none  [body(): lax.psum_scatter(local_total, 'tm', scatter_dimension=1, tiled=True)]
    gather x12 -> x0, local copies, waits for them, and re-layouts: 21.6 us -> none  [the longest x4 13.6 us: relax(): speeds = jnp.take(speed_ext, picks, axis=0)]
    slice x43 -> x0, local copies, waits for them, and re-layouts: 10.2 us -> none  [the longest x28 7.56 us: shift_east(): return jnp.concatenate([field[..., 1:], jnp.zeros_like(field[..., :1])], -1)]
    add x12 -> x0, other arithmetic: 9.91 us -> none  [the longest x4 5.51 us: relax(): updated + rows_of(sources[positions], source_width, reach).astype(jnp.flo...]
    concatenate x5 -> x0, other arithmetic: 7.96 us -> none  [the longest x1 4.99 us: with_halo(): array = jnp.concatenate([before, array, after], axis=dim)]
  transfers between devices with their start and end apart: 38 -> 0, of which waited for: 19 -> 0; matrix products, arithmetic and copies ran while one was open for 17% -> 0% of each run, Pallas kernels for 0% -> 0%
where the time goes in v1:
time: 85.8 us; the launch traced here: 85.5 us
  Pallas kernels  81.8 us (95%)
  local copies, waits for them, and re-layouts  2.96 us (3%)
    pallas_call x1, Pallas kernels, body(): pl.pallas_call(functools.partial(kernel, blocks, strips), out_shape=(jax....  81.8 us
    unnamed x4, local copies, waits for them, and re-layouts  2.96 us

profile of v1, /device:TPU:0, one launch (start us, length us, event | category | flops | bytes accessed | tf_op | source)
XLA Modules:
  0.0 85.5 jit_solution(10989291107761915385)
XLA Ops:
  0.6 81.8 %shard_map.59 = (f32[2,32,4096]{2,1,0:T(8,128)}, f32[32,1024]{1,0:T(8,128)}) custom-call(s32[32]{0:T(128)} %snap_ref.1, f32[2,32,4096]{2,1,0:T(8,128)} %guess_ref.1, bf16[8,32,4096]{2,1,0:T(8,128)(2,1)} %src_ref.1, bf16[4,2,32,4096]{3,2,1,0:T(8,128)(2,1)} %vel_ref.1), custom_call_target="tpu_custom_call" | custom-call | tf_op jit(solution)/shard_map/pallas_call | solution.py:553
  82.5 0.0 copy-start
  82.5 2.3 %copy.8 = f32[2,32,4096]{2,1,0:T(8,128)} copy(f32[2,32,4096]{2,1,0:T(8,128)} %get-tuple-element.4) | data formatting | bytes 2097152
  84.8 0.0 copy-done
  84.8 0.7 copy.9
Async XLA Ops:
  82.5 2.3 %copy-start = (f32[32,1024]{1,0:T(8,128)S(1)}, f32[32,1024]{1,0:T(8,128)}, u32[]{:S(2)}) copy-start(f32[32,1024]{1,0:T(8,128)} %get-tuple-element.5) | copy-start | bytes 393220

commit v2 on v1

--- a/solution.py
+++ b/solution.py
@@ -35,6 +35,9 @@
     edge_in,
     edge_send,
     edge_recv,
+    side_speed,
+    side_send,
+    side_recv,
     big_send,
     big_recv,
 ):
@@ -42,7 +45,9 @@
     steps = src_ref.shape[0]
     factor = steps // points
     part = cols // blocks
-    width = min(512, part)
+    width = min(1024, part)
+    deep = (gathered.shape[1] - rows) // 2
+    wide = part + 2 * LANE
     t = lax.axis_index("tm")
     s = lax.axis_index("space")
     has_up = s > 0
@@ -62,7 +67,7 @@
         pl.semaphore_signal(barrier, 1, device_id={"space": s + 1})
 
     def clear_margin(ref, size):
-        zero = jnp.zeros((rows, LANE), f32)
+        zero = jnp.zeros((ref.shape[0], LANE), f32)
         ref[:, 0:LANE] = zero
         ref[:, size - LANE : size] = zero
 
@@ -87,6 +92,9 @@
             return carry
 
         lax.fori_loop(0, rounds, zero_top, 0)
+        side_speed[0] = jnp.zeros(side_speed.shape[1:], side_speed.dtype)
+        for block in range(2, blocks):
+            gathered[block, 0:deep, LANE : LANE + wide] = jnp.zeros((deep, wide), f32)
 
     @pl.when(jnp.logical_not(has_down))
     def _():
@@ -95,6 +103,9 @@
             return carry
 
         lax.fori_loop(0, rounds, zero_bottom, 0)
+        side_speed[1] = jnp.zeros(side_speed.shape[1:], side_speed.dtype)
+        for block in range(2, blocks):
+            gathered[block, deep + rows : rows + 2 * deep, LANE : LANE + wide] = jnp.zeros((deep, wide), f32)
 
     def over_columns(fn):
         def step(k, carry):
@@ -169,23 +180,25 @@
 
     row_no = lax.broadcasted_iota(jnp.int32, (rows, 1), 0)
 
-    def stencil(src, at, vel_at, left_at, right_at, size, snap, kind, idx, edge_at):
+    def stencil(src, at, vel_at, left_at, right_at, size, snap, kind, idx, edge_at, speed_of=None):
         nu, h = kind
+        speed_of = speed_of or speed
         p = src[:, pl.ds(at, size)]
         p_left = src[:, pl.ds(at - LANE, LANE)]
         p_right = src[:, pl.ds(at + size, LANE)]
-        hay = h * speed(snap, 1, vel_at, size)
-        hay_left = h * speed(snap, 1, left_at, LANE)
-        hay_right = h * speed(snap, 1, right_at, LANE)
-        hax = h * speed(snap, 0, vel_at, size)
+        hay = h * speed_of(snap, 1, vel_at, size)
+        hay_left = h * speed_of(snap, 1, left_at, LANE)
+        hay_right = h * speed_of(snap, 1, right_at, LANE)
+        hax = h * speed_of(snap, 0, vel_at, size)
         east = jnp.concatenate([(nu + hay) * p, (nu + hay_right) * p_right], 1)
         east = pltpu.roll(east, size + LANE - 1, 1)[:, :size]
         west = jnp.concatenate([(nu - hay_left) * p_left, (nu - hay) * p], 1)
         west = pltpu.roll(west, 1, 1)[:, LANE:]
-        below = pltpu.roll((nu + hax) * p, rows - 1, 0)
-        below = jnp.where(row_no == rows - 1, edge_in[idx, 1, :, pl.ds(edge_at, size)], below)
+        below = pltpu.roll((nu + hax) * p, p.shape[0] - 1, 0)
         above = pltpu.roll((nu - hax) * p, 1, 0)
-        above = jnp.where(row_no == 0, edge_in[idx, 0, :, pl.ds(edge_at, size)], above)
+        if idx is not None:
+            below = jnp.where(row_no == rows - 1, edge_in[idx, 1, :, pl.ds(edge_at, size)], below)
+            above = jnp.where(row_no == 0, edge_in[idx, 0, :, pl.ds(edge_at, size)], above)
         return (1.0 - 4.0 * nu) * p + (east + west) + (below + above)
 
     def put_edges(value, vel_at, size, snap, kind, idx, edge_at):
@@ -215,6 +228,71 @@
     @pl.when(t > 0)
     def _():
         guess_copy().start()
+
+    vel_start = pl.multiple_of(jnp.clip(t * part - LANE, 0, cols - wide), LANE)
+
+    def to_sides(up_src, up_dst, down_src, down_dst, number):
+        return (
+            pltpu.make_async_remote_copy(
+                up_src, up_dst, side_send.at[number, 0], side_recv.at[number, 1], device_id={"space": s - 1}
+            ),
+            pltpu.make_async_remote_copy(
+                down_src, down_dst, side_send.at[number, 1], side_recv.at[number, 0], device_id={"space": s + 1}
+            ),
+        )
+
+    def speed_sides():
+        window = pl.ds(vel_start, wide)
+        return to_sides(
+            vel_ref.at[:, :, 0:16, window],
+            side_speed.at[1],
+            vel_ref.at[:, :, rows - 16 : rows, window],
+            side_speed.at[0],
+            0,
+        )
+
+    def slab_sides(block):
+        window = pl.ds(LANE, wide)
+        return to_sides(
+            gathered.at[block, deep : 2 * deep, window],
+            gathered.at[block, deep + rows : rows + 2 * deep, window],
+            gathered.at[block, rows : rows + deep, window],
+            gathered.at[block, 0:deep, window],
+            block,
+        )
+
+    def start_sides(copies):
+        up, down = copies
+
+        @pl.when(has_up)
+        def _():
+            up.start()
+
+        @pl.when(has_down)
+        def _():
+            down.start()
+
+    def wait_sides(copies):
+        up, down = copies
+
+        @pl.when(has_up)
+        def _():
+            down.wait_recv()
+
+        @pl.when(has_down)
+        def _():
+            up.wait_recv()
+
+    def sent_sides(copies):
+        up, down = copies
+
+        @pl.when(has_up)
+        def _():
+            up.wait_send()
+
+        @pl.when(has_down)
+        def _():
+            down.wait_send()
 
     def relax_chain(c, make_src, finish_last, with_residual, accumulate):
         src = make_src()
@@ -255,6 +333,8 @@
             src, idx, slot = dst, nxt, 1 - slot
             yield
 
+    lead = 2
+
     def run(chains):
         chains = list(chains)
         while chains:
@@ -299,9 +379,12 @@
 
         return finish
 
+    chains = [relax_chain(c, first_src(c), first_last(c), True, False) for c in range(points)]
     for c in range(points - 1):
-        run([relax_chain(c, first_src(c), first_last(c), True, False)])
-    run([relax_chain(points - 1, first_src(points - 1), first_last(points - 1), True, False)])
+        for _ in range(lead):
+            next(chains[c], None)
+    start_sides(speed_sides())
+    run(chains)
 
     src, idx = res_buf.at[points - 1], first_coarse
     if points > 1:
@@ -323,12 +406,10 @@
             send_edges(nxt, cols)
         src, idx = dst, nxt
 
-    wide = part + 2 * LANE
-
     def slab_copy(to, sender):
         return pltpu.make_async_remote_copy(
             b_buf.at[:, pl.ds(pl.multiple_of(to * part, LANE), wide)],
-            gathered.at[sender, :, pl.ds(LANE, wide)],
+            gathered.at[sender, deep : deep + rows, pl.ds(LANE, wide)],
             big_send.at[1, to],
             big_recv.at[1, sender],
             device_id={"tm": to},
@@ -343,21 +424,22 @@
                 slab_copy(to, t).start()
 
         for at in range(0, wide, LANE):
-            gathered[t, :, at + LANE : at + 2 * LANE] = b_buf[
+            gathered[t, deep : deep + rows, at + LANE : at + 2 * LANE] = b_buf[
                 :, pl.ds(pl.multiple_of(t * part + at, LANE), LANE)
             ]
 
     def incoming_copy(block, ref, sender):
         return pltpu.make_async_remote_copy(
-            ref.at[:, pl.ds(2 * LANE, part)],
+            ref.at[deep : deep + rows, pl.ds(2 * LANE, part)],
             incoming.at[:, pl.ds(pl.multiple_of(LANE + sender * part, LANE), part)],
             big_send.at[2, block],
             big_recv.at[2, sender],
             device_id={"tm": block},
         )
 
+    piece = min(512, part)
     pieces = [(0, LANE)]
-    pieces += [(LANE + k * width, width) for k in range(part // width)]
+    pieces += [(LANE + k * piece, piece) for k in range(part // piece)]
     pieces += [(LANE + part, LANE)]
     base = t * part - LANE
 
@@ -383,7 +465,7 @@
         def _():
             for at in range(0, part, LANE):
                 incoming[:, pl.ds(pl.multiple_of(LANE + t * part + at, LANE), LANE)] = ref[
-                    :, 2 * LANE + at : 3 * LANE + at
+                    deep : deep + rows, 2 * LANE + at : 3 * LANE + at
                 ]
 
     need(blocks - 1)
@@ -397,38 +479,52 @@
     def part_snap(block, i):
         return snap_ref[(block * points + i) * factor]
 
+    all_rows = lax.broadcasted_iota(jnp.int32, (rows + 2 * deep, 1), 0)
+    inside = jnp.logical_or(all_rows >= deep, has_up)
+    inside = jnp.logical_and(inside, jnp.logical_or(all_rows < deep + rows, has_down))
+
+    def tall_speed(snap, comp, at, size):
+        side = pl.multiple_of(at - vel_start, LANE)
+        top = side_speed[0, snap, comp, :, pl.ds(side, size)].astype(f32)[16 - deep :]
+        bottom = side_speed[1, snap, comp, :, pl.ds(side, size)].astype(f32)[:deep]
+        return jnp.concatenate([top, speed(snap, comp, at, size), bottom], 0)
+
+    def clip_side(at):
+        return pl.multiple_of(jnp.clip(base + at, vel_start, vel_start + wide - LANE), LANE)
+
+    wait_sides(speed_sides())
     if chain:
-        idx = new_edge()
-        for at, size in pieces:
-            put_edges(src[:, at + LANE : at + LANE + size], piece_vel(at, size), size, part_snap(*chain[0]), COARSE, idx, at)
-        send_edges(idx, wide)
-    for number, (block, i) in enumerate(chain):
-        more = number + 1 < len(chain)
-        nxt = new_edge() if more else None
+        for block in range(blocks - 1, 1, -1):
+            if block < blocks - 1:
+                need(block)
+            start_sides(slab_sides(block))
+        wait_sides(slab_sides(blocks - 1))
+    for block, i in chain:
         dst = solved.at[block, i % 2]
         if i == 0:
-            need(block)
-        wait_edges(idx, wide)
+            if block > 1:
+                wait_sides(slab_sides(block))
+            else:
+                need(block)
+        snap = part_snap(block, i)
         for at, size in pieces:
+            vel_at = clip_side(at) if size == LANE else piece_vel(at, size)
             new = stencil(
-                src, at + LANE, piece_vel(at, size), clip(at - LANE), clip(at + size), size,
-                part_snap(block, i), COARSE, idx, at,
+                src, at + LANE, vel_at, clip_side(at - LANE), clip_side(at + size), size,
+                snap, COARSE, None, at, tall_speed,
             )
             if i == 0:
                 new = new + gathered[block, :, at + LANE : at + LANE + size]
+            keep = inside
             if at == 0:
-                new = jnp.where(t > 0, new, 0.0)
+                keep = jnp.logical_and(inside, t > 0)
             if at == LANE + part:
-                new = jnp.where(t < blocks - 1, new, 0.0)
-            dst[:, at + LANE : at + LANE + size] = new
-            if more:
-                put_edges(new, piece_vel(at, size), size, part_snap(*chain[number + 1]), COARSE, nxt, at)
-        if more:
-            send_edges(nxt, wide)
+                keep = jnp.logical_and(inside, t < blocks - 1)
+            dst[:, at + LANE : at + LANE + size] = jnp.where(keep, new, 0.0)
         if i == 0:
             deliver(block - 1, dst)
             delivered.append((block - 1, dst))
-        src, idx = dst, nxt
+        src = dst
 
     for sender in range(blocks):
 
@@ -515,6 +611,10 @@
             def _():
                 slab_copy(to, t).wait_send()
 
+    sent_sides(speed_sides())
+    if chain:
+        for block in range(2, blocks):
+            sent_sides(slab_sides(block))
     for block, ref in delivered:
 
         @pl.when(t != block)
@@ -547,6 +647,7 @@
     factor = steps // points
     part = cols // blocks
     padded = cols + 2 * LANE
+    deep = 8 if points * (blocks - 2) <= 8 else 16
     edges = points * (2 * factor + 1) + 2 * points + points * blocks
     f32 = jnp.float32
     vmem = pl.BlockSpec(memory_space=pltpu.VMEM)
@@ -563,8 +664,8 @@
             pltpu.VMEM((rows, padded), f32),
             pltpu.VMEM((points, rows, padded), f32),
             pltpu.VMEM((rows, padded), f32),
-            pltpu.VMEM((blocks, rows, part + 4 * LANE), f32),
-            pltpu.VMEM((blocks, 2, rows, part + 4 * LANE), f32),
+            pltpu.VMEM((blocks, rows + 2 * deep, part + 4 * LANE), f32),
+            pltpu.VMEM((blocks, 2, rows + 2 * deep, part + 4 * LANE), f32),
             pltpu.VMEM((rows, padded), f32),
             pltpu.VMEM((points, rows, padded), f32),
             pltpu.VMEM((rows, cols), f32),
@@ -573,6 +674,9 @@
             pltpu.VMEM((edges, 2, 1, cols), f32),
             pltpu.SemaphoreType.DMA((edges, 2)),
             pltpu.SemaphoreType.DMA((edges, 2)),
+            pltpu.VMEM((2,) + velocity.shape[:2] + (16, part + 2 * LANE), velocity.dtype),
+            pltpu.SemaphoreType.DMA((blocks, 2)),
+            pltpu.SemaphoreType.DMA((blocks, 2)),
             pltpu.SemaphoreType.DMA((4, blocks)),
             pltpu.SemaphoreType.DMA((4, blocks)),
         ],

time: 85.8 us -> 76.5 us (0.89)
  Pallas kernels: 81.8 us -> 72.1 us
    pallas_call x1, Pallas kernels: 81.8 us -> 72.1 us  [body(): pl.pallas_call(functools.partial(kernel, blocks, strips), out_shape=(jax....]
where the time goes in v2:
time: 76.5 us; the launch traced here: 75.8 us
  Pallas kernels  72.1 us (94%)
  local copies, waits for them, and re-layouts  2.96 us (4%)
    pallas_call x1, Pallas kernels, body(): pl.pallas_call(functools.partial(kernel, blocks, strips), out_shape=(jax....  72.1 us
    unnamed x4, local copies, waits for them, and re-layouts  2.96 us

profile of v2, /device:TPU:0, one launch (start us, length us, event | category | flops | bytes accessed | tf_op | source)
XLA Modules:
  0.0 75.8 jit_solution(15313797415211453003)
XLA Ops:
  0.6 72.1 %shard_map.59 = (f32[2,32,4096]{2,1,0:T(8,128)}, f32[32,1024]{1,0:T(8,128)}) custom-call(s32[32]{0:T(128)} %snap_ref.1, f32[2,32,4096]{2,1,0:T(8,128)} %guess_ref.1, bf16[8,32,4096]{2,1,0:T(8,128)(2,1)} %src_ref.1, bf16[4,2,32,4096]{3,2,1,0:T(8,128)(2,1)} %vel_ref.1), custom_call_target="tpu_custom_call" | custom-call | tf_op jit(solution)/shard_map/pallas_call | solution.py:654
  72.8 0.0 copy-start
  72.8 2.3 %copy.8 = f32[2,32,4096]{2,1,0:T(8,128)} copy(f32[2,32,4096]{2,1,0:T(8,128)} %get-tuple-element.4) | data formatting | bytes 2097152
  75.1 0.0 copy-done
  75.1 0.7 copy.9
Async XLA Ops:
  72.8 2.3 %copy-start = (f32[32,1024]{1,0:T(8,128)S(1)}, f32[32,1024]{1,0:T(8,128)}, u32[]{:S(2)}) copy-start(f32[32,1024]{1,0:T(8,128)} %get-tuple-element.5) | copy-start | bytes 393220

commit v3 on v2

--- a/solution.py
+++ b/solution.py
@@ -125,30 +125,31 @@
     peers = blocks - 1 + jnp.minimum(s, 1) + jnp.minimum(strips - 1 - s, 1)
     pl.semaphore_wait(barrier, peers)
 
-    def edge_copies(idx, span):
-        window = pl.ds(0, span)
+    def edge_copies(idx, at):
+        window = pl.ds(at, width)
+        k = at // width
         return (
             pltpu.make_async_remote_copy(
                 edge_out.at[idx, 0, :, window],
                 edge_in.at[idx, 1, :, window],
-                edge_send.at[idx, 0],
-                edge_recv.at[idx, 1],
+                edge_send.at[idx, 0, k],
+                edge_recv.at[idx, 1, k],
                 device_id={"space": s - 1},
             ),
             pltpu.make_async_remote_copy(
                 edge_out.at[idx, 1, :, window],
                 edge_in.at[idx, 0, :, window],
-                edge_send.at[idx, 1],
-                edge_recv.at[idx, 0],
+                edge_send.at[idx, 1, k],
+                edge_recv.at[idx, 0, k],
                 device_id={"space": s + 1},
             ),
         )
 
-    used = []
-
-    def send_edges(idx, span):
-        used.append((idx, span))
-        up, down = edge_copies(idx, span)
+    used = set()
+
+    def send_edges(idx, at):
+        used.add(idx)
+        up, down = edge_copies(idx, at)
 
         @pl.when(has_up)
         def _():
@@ -158,8 +159,8 @@
         def _():
             down.start()
 
-    def wait_edges(idx, span):
-        up, down = edge_copies(idx, span)
+    def wait_edges(idx, at):
+        up, down = edge_copies(idx, at)
 
         @pl.when(has_up)
         def _():
@@ -207,11 +208,13 @@
         last = vel_ref[snap, 0, rows - 16 : rows, pl.ds(vel_at, size)].astype(f32)[15:16]
         edge_out[idx, 0, :, pl.ds(edge_at, size)] = (nu + h * first) * value[0:1]
         edge_out[idx, 1, :, pl.ds(edge_at, size)] = (nu - h * last) * value[rows - 1 : rows]
+        send_edges(idx, edge_at)
 
     def snap_at(local):
         return snap_ref[t * steps + local]
 
     def full_stencil(src, at, snap, kind, idx):
+        wait_edges(idx, at)
         left = pl.multiple_of(jnp.maximum(at - LANE, 0), LANE)
         right = pl.multiple_of(jnp.minimum(at + width, cols - LANE), LANE)
         return stencil(src, at + LANE, at, left, right, width, snap, kind, idx, at)
@@ -303,7 +306,6 @@
             put_edges(src[:, pl.ds(at + LANE, width)], at, width, snap, FINE, idx, at)
 
         over_columns(first)
-        send_edges(idx, cols)
         yield
         slot = 1
         last = 0 if with_residual else 1
@@ -314,7 +316,6 @@
             more = offset > last
             nxt = new_edge() if more else None
             snap_next = snap_at(n - 1) if more else None
-            wait_edges(idx, cols)
 
             def work(at, src=src, dst=dst, idx=idx, nxt=nxt, snap=snap, snap_next=snap_next, n=n, offset=offset, more=more):
                 new = full_stencil(src, at, snap, FINE, idx)
@@ -324,16 +325,16 @@
                     dst[:, pl.ds(at + LANE, width)] = new
                 if accumulate:
                     total[:, pl.ds(at, width)] += new
+                if accumulate and not more and c == 0:
+                    leave(at)
                 if offset == 0:
                     finish_last(at, new)
 
             over_columns(work)
-            if more:
-                send_edges(nxt, cols)
             src, idx, slot = dst, nxt, 1 - slot
             yield
 
-    lead = 2
+    lead = 1
 
     def run(chains):
         chains = list(chains)
@@ -387,12 +388,9 @@
     run(chains)
 
     src, idx = res_buf.at[points - 1], first_coarse
-    if points > 1:
-        send_edges(idx, cols)
     for i in range(points - 2, -1, -1):
         nxt = new_edge() if i > 0 else None
         dst = b_buf if i == 0 else x_buf.at[0, i % 2]
-        wait_edges(idx, cols)
 
         def condense(at, src=src, dst=dst, idx=idx, nxt=nxt, i=i):
             new = full_stencil(src, at, snap_coarse[i], COARSE, idx)
@@ -402,8 +400,6 @@
                 put_edges(new, at, width, snap_coarse[i - 1], COARSE, nxt, at)
 
         over_columns(condense)
-        if i > 0:
-            send_edges(nxt, cols)
         src, idx = dst, nxt
 
     def slab_copy(to, sender):
@@ -526,30 +522,50 @@
             delivered.append((block - 1, dst))
         src = dst
 
-    for sender in range(blocks):
-
+    def total_copy(to, sender):
+        return pltpu.make_async_remote_copy(
+            total.at[:, pl.ds(pl.multiple_of(to * part, LANE), part)],
+            totals_in.at[sender],
+            big_send.at[3, to],
+            big_recv.at[3, sender],
+            device_id={"tm": to},
+        )
+
+    def leave(at):
+        if width == part:
+            to = at // width
+
+            @pl.when(t != to)
+            def _():
+                total_copy(to, t).start()
+
+    def arrived(sender):
         @pl.when(jnp.logical_and(t < blocks - 1, t != sender))
         def _():
             incoming_copy(t, gathered.at[0], sender).wait_recv()
+
+    if width != part:
+        for sender in range(blocks):
+            arrived(sender)
 
     ready = set()
     idx_corr = new_edge()
 
     def start_all(at):
+        if width == part:
+            arrived(at // width)
         value = incoming[:, pl.ds(at + LANE, width)]
         put_edges(value, at, width, snap_coarse[points - 1], COARSE, idx_corr, at)
         x_buf[points - 1, 0, :, pl.ds(at + LANE, width)] = value + next_guess[:, pl.ds(at + LANE, width)]
         total[:, pl.ds(at, width)] = jnp.zeros((rows, width), f32)
 
     over_columns(start_all)
-    send_edges(idx_corr, cols)
 
     def correction_chain():
         src, idx = incoming, idx_corr
         for i in range(points - 1, -1, -1):
             nxt = new_edge() if i > 0 else None
             dst = corr_buf.at[i]
-            wait_edges(idx, cols)
 
             def work(at, src=src, dst=dst, idx=idx, nxt=nxt, i=i):
                 new = full_stencil(src, at, snap_coarse[i], COARSE, idx)
@@ -564,7 +580,6 @@
 
             over_columns(work)
             if i > 0:
-                send_edges(nxt, cols)
                 ready.add(i - 1)
             src, idx = dst, nxt
             yield
@@ -576,31 +591,26 @@
 
     run([second_chain(points - 1), correction_chain()] + [second_chain(c) for c in range(points - 2, -1, -1)])
 
-    def total_copy(to, sender):
-        return pltpu.make_async_remote_copy(
-            total.at[:, pl.ds(pl.multiple_of(to * part, LANE), part)],
-            totals_in.at[sender],
-            big_send.at[3, to],
-            big_recv.at[3, sender],
-            device_id={"tm": to},
-        )
-
-    for to in range(blocks):
-
-        @pl.when(t != to)
-        def _():
-            total_copy(to, t).start()
-
-    for idx, span in used:
-        up, down = edge_copies(idx, span)
-
-        @pl.when(has_up)
-        def _():
-            up.wait_send()
-
-        @pl.when(has_down)
-        def _():
-            down.wait_send()
+    if width != part:
+        for to in range(blocks):
+
+            @pl.when(t != to)
+            def _():
+                total_copy(to, t).start()
+
+    def edges_sent(at):
+        for idx in sorted(used):
+            up, down = edge_copies(idx, at)
+
+            @pl.when(has_up)
+            def _():
+                up.wait_send()
+
+            @pl.when(has_down)
+            def _():
+                down.wait_send()
+
+    over_columns(edges_sent)
 
     @pl.when(t > 0)
     def _():
@@ -672,8 +682,8 @@
             pltpu.VMEM((blocks, rows, part), f32),
             pltpu.VMEM((edges, 2, 1, cols), f32),
             pltpu.VMEM((edges, 2, 1, cols), f32),
-            pltpu.SemaphoreType.DMA((edges, 2)),
-            pltpu.SemaphoreType.DMA((edges, 2)),
+            pltpu.SemaphoreType.DMA((edges, 2, blocks * max(1, part // 1024))),
+            pltpu.SemaphoreType.DMA((edges, 2, blocks * max(1, part // 1024))),
             pltpu.VMEM((2,) + velocity.shape[:2] + (16, part + 2 * LANE), velocity.dtype),
             pltpu.SemaphoreType.DMA((blocks, 2)),
             pltpu.SemaphoreType.DMA((blocks, 2)),

time: 76.5 us -> 75.1 us (0.982)
  Pallas kernels: 72.1 us -> 70.7 us
    pallas_call x1, Pallas kernels: 72.1 us -> 70.7 us  [body(): pl.pallas_call(functools.partial(kernel, blocks, strips), out_shape=(jax....]
where the time goes in v3:
time: 75.1 us; the launch traced here: 74.3 us
  Pallas kernels  70.7 us (94%)
  local copies, waits for them, and re-layouts  2.96 us (4%)
    pallas_call x1, Pallas kernels, body(): pl.pallas_call(functools.partial(kernel, blocks, strips), out_shape=(jax....  70.7 us
    unnamed x4, local copies, waits for them, and re-layouts  2.96 us

profile of v3, /device:TPU:0, one launch (start us, length us, event | category | flops | bytes accessed | tf_op | source)
XLA Modules:
  0.0 74.3 jit_solution(3530394753758859962)
XLA Ops:
  0.6 70.7 %shard_map.59 = (f32[2,32,4096]{2,1,0:T(8,128)}, f32[32,1024]{1,0:T(8,128)}) custom-call(s32[32]{0:T(128)} %snap_ref.1, f32[2,32,4096]{2,1,0:T(8,128)} %guess_ref.1, bf16[8,32,4096]{2,1,0:T(8,128)(2,1)} %src_ref.1, bf16[4,2,32,4096]{3,2,1,0:T(8,128)(2,1)} %vel_ref.1), custom_call_target="tpu_custom_call" | custom-call | tf_op jit(solution)/shard_map/pallas_call | solution.py:664
  71.3 0.0 copy-start
  71.3 2.3 %copy.8 = f32[2,32,4096]{2,1,0:T(8,128)} copy(f32[2,32,4096]{2,1,0:T(8,128)} %get-tuple-element.4) | data formatting | bytes 2097152
  73.6 0.0 copy-done
  73.6 0.7 copy.9
Async XLA Ops:
  71.3 2.3 %copy-start = (f32[32,1024]{1,0:T(8,128)S(1)}, f32[32,1024]{1,0:T(8,128)}, u32[]{:S(2)}) copy-start(f32[32,1024]{1,0:T(8,128)} %get-tuple-element.5) | copy-start | bytes 393220
